TPU v7x, 32 devices: a whole 2x2x4 slice. The times are simulated.
32 devices in a mesh: seq: 8 (over z, y), head: 4 (over x, core).
Axes of the slice: x: 2, y: 2, z: 4, core: 2. Of those that a mesh axis runs over, the one named last changes fastest.
Arguments:
- tokens: bfloat16 [4096, 4096], P('seq'), may hold values from -6 to 6
- w_query: bfloat16 [4096, 2048], P('seq', 'head'), may hold values from -0.09375 to 0.09375
- w_key: bfloat16 [4096, 2048], P('seq', 'head'), may hold values from -0.09375 to 0.09375
- w_value: bfloat16 [4096, 2048], P('seq', 'head'), may hold values from -0.09375 to 0.09375
- omega_seed: int32 [16, 128, 256], P('head'), may hold values from -4 to 4
- grad_out: bfloat16 [4096, 2048], P('seq', 'head'), may hold values from -6 to 6
Outputs:
- input_grad: bfloat16 [4096, 4096], P('seq', 'head')
- query_wgrad: float32 [4096, 2048], P('seq', 'head')
- key_wgrad: float32 [4096, 2048], P('seq', 'head')
- value_wgrad: float32 [4096, 2048], P('seq', 'head')
Inputs may be any that keep to these rules, and one draw needn't show every extreme that they name: `omega_seed`: the feature seeds are small whole numbers.
All inputs are finite; a program needn't handle non-finite values.
Results may differ from a plain program's by a relative error of at most 0.02.
Values may be sent and summed in bfloat16 or wider, within the bound.
A program may use at most 128 MiB of HBM per device.

v0:
```python
import math

import jax
import jax.numpy as jnp
from jax import lax
from jax.sharding import PartitionSpec as P

exact_arithmetic_mode = lax.Precision.HIGHEST
seed_step = 0.4


def carried_in(shard, axis, join, neutral):
    place = lax.axis_index(axis)
    gathered = jax.tree.map(
        lambda a, kind: lax.all_gather(a.astype(kind), axis), shard, (jnp.bfloat16, jnp.bfloat16)
    )
    state = jax.tree.map(lambda a, e: jnp.zeros_like(a) + jnp.asarray(e, a.dtype), shard, neutral)

    def one(hop, state):
        return join(
            state,
            jax.tree.map(
                lambda a, own: lax.dynamic_index_in_dim(a, hop, 0, False).astype(own.dtype),
                gathered,
                shard,
            ),
        )

    return lax.fori_loop(0, place, one, state)


def carried_in_2(shard, axis, join, neutral):
    count = lax.axis_size(axis)
    place = lax.axis_index(axis)
    ahead = count - 1 - place
    gathered = jax.tree.map(
        lambda a, kind: lax.all_gather(a.astype(kind), axis),
        shard,
        jax.tree.map(lambda a: jnp.bfloat16 if a.dtype == jnp.float32 else a.dtype, shard),
    )
    state = jax.tree.map(lambda a, e: jnp.zeros_like(a) + jnp.asarray(e, a.dtype), shard, neutral)

    def one(hop, state):
        source = count - 1 - hop
        return join(
            state,
            jax.tree.map(
                lambda a, own: lax.dynamic_index_in_dim(a, source, 0, False).astype(own.dtype),
                gathered,
                shard,
            ),
        )

    return lax.fori_loop(0, ahead, one, state)


def feature_map(scaled, projection):
    projected = jnp.einsum("htd,hdm->htm", scaled, projection, precision=exact_arithmetic_mode)
    return jnp.exp(projected - 0.5 * jnp.sum(scaled * scaled, -1, keepdims=True)) / math.sqrt(
        projection.shape[-1]
    )


def feature_grad(upstream, features, scaled, projection):
    weighted = upstream * features
    projected = jnp.einsum("htm,hdm->htd", weighted, projection, precision=exact_arithmetic_mode)
    return (projected - jnp.sum(weighted, -1, keepdims=True) * scaled) * scaled.shape[-1] ** (-0.25)


def add_states(earlier, later_part):
    return (earlier[0] + later_part[0], earlier[1] + later_part[1])


def head_major(value_matrix, heads_here):
    tok_rows = value_matrix.shape[0]
    return value_matrix.astype(jnp.float32).reshape(tok_rows, heads_here, -1).transpose(1, 0, 2)


def token_major(value_matrix):
    return value_matrix.transpose(1, 0, 2).reshape(value_matrix.shape[1], -1).astype(jnp.bfloat16)


def back_product(grads, weight):
    return lax.dot_general(
        grads, weight, (((1,), (1,)), ((), ())), preferred_element_type=jnp.float32
    )


def projection_term(tokens, grads):
    return lax.dot_general(
        tokens, grads, (((0,), (0,)), ((), ())), preferred_element_type=jnp.float32
    )


def per_device(tokens, w_query, w_key, w_value, omega_seed, grad_out):
    heads_here = omega_seed.shape[0]
    head_size = omega_seed.shape[1]
    full_query, full_key, full_value = (
        lax.all_gather(w_query, "seq", axis=0, tiled=True),
        lax.all_gather(w_key, "seq", axis=0, tiled=True),
        lax.all_gather(w_value, "seq", axis=0, tiled=True),
    )
    query_act = jnp.dot(tokens, full_query, preferred_element_type=jnp.float32).astype(jnp.bfloat16)
    key_act = jnp.dot(tokens, full_key, preferred_element_type=jnp.float32).astype(jnp.bfloat16)
    value_act = jnp.dot(tokens, full_value, preferred_element_type=jnp.float32).astype(jnp.bfloat16)
    projection = omega_seed.astype(jnp.float32) * seed_step
    scale_in = head_size ** (-0.25)
    query_scaled = head_major(query_act, heads_here) * scale_in
    key_scaled = head_major(key_act, heads_here) * scale_in
    value_matrix = head_major(value_act, heads_here)
    upstream = head_major(grad_out, heads_here)
    query_feature_rows = feature_map(query_scaled, projection)
    source_embedding_entries = feature_map(key_scaled, projection)
    tok_rows = tokens.shape[0]
    causal = jnp.tril(jnp.ones((tok_rows, tok_rows), jnp.float32))
    block_local_states = jnp.einsum(
        "vzn,vza->vna", source_embedding_entries, value_matrix, precision=exact_arithmetic_mode
    )
    local_totals = jnp.sum(source_embedding_entries, 1)
    zero_states = jnp.zeros_like(block_local_states)
    zero_totals = jnp.zeros_like(local_totals)
    prefix_carried_outer, prefix_normaliser_accrual = carried_in(
        (block_local_states, local_totals), "seq", add_states, (zero_states, zero_totals)
    )
    attention_scores = (
        jnp.einsum(
            "htm,hsm->hts",
            query_feature_rows,
            source_embedding_entries,
            precision=exact_arithmetic_mode,
        )
        * causal
    )
    attention_numerator = jnp.einsum(
        "xyw,xwc->xyc", attention_scores, value_matrix, precision=exact_arithmetic_mode
    ) + jnp.einsum(
        "sji,six->sjx", query_feature_rows, prefix_carried_outer, precision=exact_arithmetic_mode
    )
    normer = jnp.sum(attention_scores, -1) + jnp.einsum(
        "htm,hm->ht", query_feature_rows, prefix_normaliser_accrual, precision=exact_arithmetic_mode
    )
    output = attention_numerator / normer[..., None]
    dividend_cotangent = upstream / normer[..., None]
    normaliser_cotangent = -jnp.sum(upstream * output, -1) / normer
    couplewise_products = (
        jnp.einsum(
            "htd,hsd->hts", dividend_cotangent, value_matrix, precision=exact_arithmetic_mode
        )
        + normaliser_cotangent[..., None]
    ) * causal
    target_embedding_cotangent = (
        jnp.einsum(
            "mez,mzo->meo",
            couplewise_products,
            source_embedding_entries,
            precision=exact_arithmetic_mode,
        )
        + jnp.einsum(
            "zrc,zfc->zrf",
            dividend_cotangent,
            prefix_carried_outer,
            precision=exact_arithmetic_mode,
        )
        + normaliser_cotangent[..., None] * prefix_normaliser_accrual[:, None, :]
    )
    query16 = token_major(
        feature_grad(target_embedding_cotangent, query_feature_rows, query_scaled, projection)
    )
    subsequent_local_states = jnp.einsum(
        "opu,opc->ouc", query_feature_rows, dividend_cotangent, precision=exact_arithmetic_mode
    )
    later_totals = jnp.einsum(
        "htm,ht->hm", query_feature_rows, normaliser_cotangent, precision=exact_arithmetic_mode
    )
    subsequent_states, subsequent_sum = carried_in_2(
        (subsequent_local_states, later_totals), "seq", add_states, (zero_states, zero_totals)
    )
    key_feature_gradient = (
        jnp.einsum(
            "ykl,yku->ylu", couplewise_products, query_feature_rows, precision=exact_arithmetic_mode
        )
        + jnp.einsum(
            "bgq,bxq->bgx", value_matrix, subsequent_states, precision=exact_arithmetic_mode
        )
        + subsequent_sum[:, None, :]
    )
    value_gradient_rows = jnp.einsum(
        "vkm,vky->vmy", attention_scores, dividend_cotangent, precision=exact_arithmetic_mode
    ) + jnp.einsum(
        "tjr,tro->tjo", source_embedding_entries, subsequent_states, precision=exact_arithmetic_mode
    )
    key16 = token_major(
        feature_grad(key_feature_gradient, source_embedding_entries, key_scaled, projection)
    )
    value16 = token_major(value_gradient_rows)
    joined = jnp.concatenate([query16, key16, value16], 1)
    weight_total = lax.psum_scatter(
        projection_term(tokens, joined).astype(jnp.bfloat16), "seq", scatter_dimension=0, tiled=True
    ).astype(jnp.float32)
    columns = query16.shape[1]
    query_wgrad = weight_total[:, :columns]
    key_wgrad = weight_total[:, columns : 2 * columns]
    value_wgrad = weight_total[:, 2 * columns :]
    partial_input = (
        back_product(query16, full_query)
        + back_product(key16, full_key)
        + back_product(value16, full_value)
    )
    input_grad = lax.psum_scatter(
        partial_input.astype(jnp.bfloat16), "head", scatter_dimension=1, tiled=True
    )
    return (input_grad, query_wgrad, key_wgrad, value_wgrad)


def solution(mesh):
    placed = (
        P("seq", None),
        P("seq", "head"),
        P("seq", "head"),
        P("seq", "head"),
        P("head", None, None),
        P("seq", "head"),
    )
    return jax.shard_map(
        per_device,
        mesh=mesh,
        in_specs=placed,
        out_specs=(P("seq", "head"), P("seq", "head"), P("seq", "head"), P("seq", "head")),
        check_vma=False,
    )
```

profile of v0, /device:TPU:0, one launch (start us, length us, event | category | flops | bytes accessed | tf_op | source)
XLA Modules:
  0.0 653.2 jit_solution(7130954048642170528)
XLA Ops:
  9.4 76.8 %all-gather.16.cloned.1.call-done = bf16[4096,512]{1,0:T(8,128)(2,1)} async-done(((bf16[512,512]{1,0:T(8,128)(2,1)}), bf16[4096,512]{1,0:T(8,128)(2,1)}) %all-gather.16.cloned.1.call-update) | async-done | bytes 4194320 | tf_op jit(solution)/shard_map/all_gather | solution.py:101
  86.3 5.8 convolution_convert_fusion.1
  93.2 66.9 %all-gather.14.cloned.1.call-done = bf16[4096,512]{1,0:T(8,128)(2,1)} async-done(((bf16[512,512]{1,0:T(8,128)(2,1)}), bf16[4096,512]{1,0:T(8,128)(2,1)}) %all-gather.14.cloned.1.call-update) | async-done | bytes 4194320 | tf_op jit(solution)/shard_map/all_gather | solution.py:100
  160.1 5.8 convolution_convert_fusion.2
  172.9 26.6 %all-gather.4 = bf16[8,4,256]{2,1,0:T(4,128)(2,1)S(1)} all-gather(bf16[1,4,256]{2,1,0:T(4,128)(2,1)S(1)} %bitcast.156), channel_id=3, replica_groups=mesh['seq'=8,'head'=4] {'seq'}, dimensions={0}, use_global_device_ids=true | all-gather | bytes 18432 | tf_op jit(solution)/shard_map/all_gather | solution.py:15
  199.5 34.7 %all-gather.12.cloned.1.call-done = bf16[4096,512]{1,0:T(8,128)(2,1)} async-done(((bf16[512,512]{1,0:T(8,128)(2,1)}), bf16[4096,512]{1,0:T(8,128)(2,1)}) %all-gather.12.cloned.1.call-update) | async-done | bytes 4194320 | tf_op jit(solution)/shard_map/all_gather | solution.py:99
  234.2 5.9 convolution_convert_fusion.3
  242.4 5.2 multiply_reduce_fusion
  247.6 36.7 %all-gather.18.cloned.1.call-done = bf16[32,256,128]{2,1,0:T(8,128)(2,1)} async-done(((bf16[4,256,128]{2,1,0:T(8,128)(2,1)}), bf16[32,256,128]{2,1,0:T(8,128)(2,1)}) %all-gather.18.cloned.1.call-update) | async-done | bytes 2097168 | tf_op jit(solution)/shard_map/all_gather | solution.py:15
  286.4 3.9 convolution_convert_fusion.4
  290.4 2.6 fusion.77
  293.0 4.1 fusion.39
  299.0 45.9 %all-gather.5 = bf16[8,4,256]{2,1,0:T(4,128)(2,1)S(1)} all-gather(bf16[1,4,256]{2,1,0:T(4,128)(2,1)S(1)} %bitcast.155), channel_id=5, replica_groups=mesh['seq'=8,'head'=4] {'seq'}, dimensions={0}, use_global_device_ids=true | all-gather | bytes 18432 | tf_op jit(solution)/shard_map/all_gather | solution.py:37
  346.9 4.3 fusion.2
  355.8 5.7 fusion.1
  361.6 7.8 %while.27 = (s32[]{:T(128)}, f32[4,256,128]{2,1,0:T(8,128)S(1)}, f32[4,256]{1,0:T(4,128)S(1)}, s32[]{:T(128)}, bf16[8,4,256,128]{3,2,1,0:T(8,128)(2,1)}, /*index...) while((s32[]{:T(128)}, f32[4,256,128]{2,1,0:T(8,128)S(1)}, ...), condition=%wide.region_9.10_spmd, body=%wide.region_8.9_spmd.sunk | while | flops 264198 | bytes 1321115 | solution.py:54
  369.4 3.1 fusion.80
  372.5 7.0 %fusion.30 = bf16[4,512,128]{1,2,0:T(8,128)(2,1)S(1)} fusion(f32[4,512,128]{1,2,0:T(8,128)S(1)} %fusion.80, f32[4,512,512]{1,2,0:T(8,128)} %get-tuple-element.159, f32[512,512]{0,1:T(8,128)S(1)} %fusion.50, f32[4,512]{1,0:T(4,128)S(1)} %bitcast_add_fusion, f32[512,512]{0,1:T(8,128)S(1)} %copy-done.6), kind=kOutput, calls=%fused_computation.44 | convolution fusion | flops 1612447744 | bytes 7872512 | tf_op jit(solution)/shard_map/vkm,vky->vmy/dot_general | solution.py:187
  382.4 11.4 %fusion = bf16[4096,1536]{0,1:T(8,128)(2,1)} fusion(bf16[512,4096]{1,0:T(8,128)(2,1)S(1)} %copy-done.25, bf16[512,512]{0,1:T(8,128)(2,1)S(1)} %bitcast.145, bf16[512,512]{0,1:T(8,128)(2,1)S(1)} %bitcast.147, bf16[512,512]{0,1:T(8,128)(2,1)S(1)} %bitcast.143), kind=kOutput, calls=%fused_computation.5 | convolution fusion | flops 6453460992 | bytes 18350080 | tf_op jit(solution)/shard_map/dot_general | solution.py:90
  394.1 4.7 fusion.78
  398.9 5.6 fusion.79
  404.5 7.8 %add_convert_fusion = bf16[512,4096]{1,0:T(8,128)(2,1)} fusion(f32[512,4096]{1,0:T(8,128)S(1)} %fusion.78, f32[512,4096]{1,0:T(8,128)} %fusion.79, bf16[512,512]{0,1:T(8,128)(2,1)S(1)} %bitcast.146, bf16[4096,512]{1,0:T(8,128)(2,1)S(1)} %copy-done.19), kind=kOutput, calls=%fused_computation.6 | convolution fusion | flops 2153775104 | bytes 25690112 | tf_op jit(solution)/shard_map/dot_general | solution.py:84
  412.3 186.8 %reduce-scatter.5.cloned.1.call-done = bf16[512,1536]{0,1:T(8,128)(2,1)} async-done(((bf16[4096,1536]{0,1:T(8,128)(2,1)}), bf16[512,1536]{0,1:T(8,128)(2,1)}) %reduce-scatter.5.cloned.1.call-update) | async-done | bytes 1572880 | tf_op jit(solution)/shard_map/reduce_scatter | solution.py:197
  604.9 41.0 %reduce-scatter.3.cloned.1.call-done = bf16[512,1024]{1,0:T(8,128)(2,1)} async-done(((bf16[512,4096]{1,0:T(8,128)(2,1)}), bf16[512,1024]{1,0:T(8,128)(2,1)}) %reduce-scatter.3.cloned.1.call-update) | async-done | bytes 1048592 | tf_op jit(solution)/shard_map/reduce_scatter | solution.py:209
  (112 shorter events, 39.3 us)
Async XLA Ops:
  7.2 79.1 %all-gather.16.cloned.1.call-start = ((), (), s32[]{:S(2)}) async-start(), calls=%async_computation.4 | async-start | bytes 4718592 | tf_op jit(solution)/shard_map/all_gather | solution.py:101
  7.9 152.2 %all-gather.14.cloned.1.call-start = ((), (), s32[]{:S(2)}) async-start(), calls=%async_computation.3 | async-start | bytes 4718592 | tf_op jit(solution)/shard_map/all_gather | solution.py:100
  8.6 225.6 %all-gather.12.cloned.1.call-start = ((), (), s32[]{:S(2)}) async-start(), calls=%async_computation.2 | async-start | bytes 4718592 | tf_op jit(solution)/shard_map/all_gather | solution.py:99
  9.4 274.9 %all-gather.18.cloned.1.call-start = ((), (), s32[]{:S(2)}) async-start(), calls=%async_computation.7 | async-start | bytes 2359296 | tf_op jit(solution)/shard_map/all_gather | solution.py:15
  93.2 75.2 %copy-start.12 = (bf16[512,4,128]{2,0,1:T(8,128)(2,1)}, bf16[512,4,128]{2,0,1:T(8,128)(2,1)S(1)}, u32[]{:S(2)}) copy-start(bf16[512,4,128]{2,0,1:T(8,128)(2,1)S(1)} %copy.43) | copy-start | bytes 1572868
  93.2 72.9 %copy-start.7 = (s32[4,128,256]{2,1,0:T(8,128)S(1)}, s32[4,128,256]{2,1,0:T(8,128)}, u32[]{:S(2)}) copy-start(s32[4,128,256]{2,1,0:T(8,128)} %param.14) | copy-start | bytes 1572868
  165.9 2.5 copy-start.15
  166.1 5.5 copy-start.24
  171.6 189.9 %all-gather.20.cloned.1.call-start = ((), (), s32[]{:S(2)}) async-start(), calls=%async_computation.8 | async-start | bytes 2359296 | tf_op jit(solution)/shard_map/all_gather | solution.py:37
  234.2 6.1 copy-start.8
  290.3 308.9 %reduce-scatter.5.cloned.1.call-start = ((), (), s32[]{:S(2)}) async-start(), calls=%async_computation.6 | async-start | bytes 14155776 | tf_op jit(solution)/shard_map/reduce_scatter | solution.py:197
  290.4 2.6 copy-start.5
  290.4 2.6 copy-start.23
  293.0 52.0 %copy-start.13 = (bf16[512,4,128]{2,0,1:T(8,128)(2,1)S(1)}, bf16[512,4,128]{2,0,1:T(8,128)(2,1)}, u32[]{:S(2)}) copy-start(bf16[512,4,128]{2,0,1:T(8,128)(2,1)} %copy-done.12) | copy-start | bytes 1572868
  299.0 47.8 %copy-start.2 = (f32[4,512,256]{1,2,0:T(8,128)S(1)}, f32[4,512,256]{1,2,0:T(8,128)}, u32[]{:S(2)}) copy-start(f32[4,512,256]{1,2,0:T(8,128)} %copy-done) | copy-start | bytes 6291460
  346.9 4.3 copy-start.4
  369.4 3.1 copy-start.6
  372.5 7.0 %copy-start.3 = (f32[4,512,256]{1,2,0:T(8,128)S(1)}, f32[4,512,256]{1,2,0:T(8,128)}, u32[]{:S(2)}) copy-start(f32[4,512,256]{1,2,0:T(8,128)} %copy-done) | copy-start | bytes 6291460
  372.5 7.0 %copy-start.11 = (f32[4,512,256]{1,2,0:T(8,128)S(1)}, f32[4,512,256]{1,2,0:T(8,128)}, u32[]{:S(2)}) copy-start(f32[4,512,256]{1,2,0:T(8,128)} %fusion.1) | copy-start | bytes 6291460
  372.5 7.0 %copy-start.14 = (bf16[512,4,128]{2,0,1:T(8,128)(2,1)S(1)}, bf16[512,4,128]{2,0,1:T(8,128)(2,1)}, u32[]{:S(2)}) copy-start(bf16[512,4,128]{2,0,1:T(8,128)(2,1)} %copy-done.12) | copy-start | bytes 1572868
  379.6 2.8 copy-start.25
  393.8 252.1 %reduce-scatter.3.cloned.1.call-start = ((), (), s32[]{:S(2)}) async-start(), calls=%async_computation.5 | async-start | bytes 5242880 | tf_op jit(solution)/shard_map/reduce_scatter | solution.py:209
  394.1 4.8 copy-start.20
  398.9 5.6 copy-start.19
  (9 other events, 15.7 us)
Sparse Core Ops, SparseCore 0:
  10.1 76.0 all-gather.15
  88.4 71.6 all-gather.13
  162.2 71.9 all-gather.11
  236.8 47.5 all-gather.17
  290.4 61.6 all-gather.19
  393.9 205.2 reduce-scatter.4
  602.3 43.5 reduce-scatter.2
where the time goes:
time: 660 us; the launch traced here: 653 us
  waiting for transfers between devices  445 us (67%)
  matrix products  101 us (15%)
  blocking collectives  72.5 us (11%)
  between operations  15.1 us (2%)
  local copies, waits for them, and re-layouts  10.3 us (2%)
  other arithmetic  8.05 us (1%)
    reduce_scatter x1, waiting for transfers between devices, per_device(): lax.psum_scatter(projection_term(tokens, joined).astype(jnp.bfloat16), 's...  187 us
    all_gather x1, waiting for transfers between devices, per_device(): lax.all_gather(w_value, 'seq', axis=0, tiled=True)  76.8 us
    all_gather x1, waiting for transfers between devices, per_device(): lax.all_gather(w_key, 'seq', axis=0, tiled=True)  66.9 us
    all_gather x1, blocking collectives, carried_in_2(): lax.all_gather(a.astype(kind), axis)  45.9 us
    reduce_scatter x1, waiting for transfers between devices, per_device(): lax.psum_scatter(partial_input.astype(jnp.bfloat16), 'head', scatter_dime...  41 us
    all_gather x1, waiting for transfers between devices, carried_in(): lax.all_gather(a.astype(kind), axis)  36.7 us
    all_gather x1, waiting for transfers between devices, per_device(): lax.all_gather(w_query, 'seq', axis=0, tiled=True)  34.7 us
    all_gather x1, blocking collectives, carried_in(): lax.all_gather(a.astype(kind), axis)  26.6 us
  transfers between devices with their start and end apart: 7, of which 6 were waited for; matrix products, arithmetic and copies ran while one was open for 12% of the time, Pallas kernels for 0%

commit v1 on v0

v1 whole, which is shorter than its diff:
```python
import functools
import math

import jax
import jax.numpy as jnp
from jax import lax
from jax.experimental import pallas as pl
from jax.experimental.pallas import tpu as pltpu
from jax.sharding import PartitionSpec as P

seed_step = 0.4
MESH = pl.DeviceIdType.MESH
VMEM = pl.BlockSpec(memory_space=pltpu.VMEM)


def ein(spec, a, b):
    return jnp.einsum(
        spec,
        a.astype(jnp.bfloat16),
        b.astype(jnp.bfloat16),
        preferred_element_type=jnp.float32,
    )


def ring_index(pos, n):
    pos = lax.rem(pos + 2 * n, n)
    odd = lax.div(pos, n // 2)
    return (1 - odd) * (2 * pos) + odd * (2 * (n - 1 - pos) + 1)


def ring_pos(index, n):
    odd = lax.rem(index, 2)
    half = lax.div(index, 2)
    return (1 - odd) * half + odd * (n - 1 - half)


def greet_ring(ahead, behind, others):
    barrier = pltpu.get_barrier_semaphore()
    for device in ({"seq": ahead}, {"seq": behind}):
        pl.semaphore_signal(barrier, inc=1, device_id=device, device_id_type=MESH)
    for device in others:
        pl.semaphore_signal(barrier, inc=1, device_id=device, device_id_type=MESH)
    pl.semaphore_wait(barrier, 2 + len(others))


def project_kernel(n, tok_ref, w_ref, act_ref, full_ref, acc, local_sem, send_sem, recv_sem):
    me = lax.axis_index("seq")
    place = ring_pos(me, n)
    ahead, behind = ring_index(place + 1, n), ring_index(place - 1, n)
    rows = w_ref.shape[1]
    greet_ring(ahead, behind, ())
    own = pltpu.make_async_copy(w_ref, full_ref.at[:, me], local_sem)
    own.start()
    acc[...] = jnp.zeros_like(acc)
    own.wait()

    def owner_of(way, step):
        return ring_index(place - step if way == 0 else place + step, n)

    def multiply(step):
        for way in range(2):
            owner = owner_of(way, step)
            columns = pl.ds(pl.multiple_of(owner * rows, rows), rows)
            acc[way] += jnp.dot(
                tok_ref[:, columns], full_ref[way, owner], preferred_element_type=jnp.float32
            )

    def one(step, carry):
        copies = []
        for way, target in ((0, ahead), (1, behind)):
            owner = owner_of(way, step)
            copies.append(
                pltpu.make_async_remote_copy(
                    src_ref=full_ref.at[way, owner],
                    dst_ref=full_ref.at[way, owner],
                    send_sem=send_sem.at[way, step],
                    recv_sem=recv_sem.at[way, step],
                    device_id={"seq": target},
                    device_id_type=MESH,
                )
            )
        for copy in copies:
            copy.start()
        multiply(step)
        for copy in copies:
            copy.wait()
        return carry

    lax.fori_loop(0, n - 1, one, 0)
    multiply(n - 1)
    act_ref[...] = acc[...].astype(act_ref.dtype)


def project(tokens, weights, n):
    ways, rows, width = weights.shape
    toks = tokens.shape[0]
    return pl.pallas_call(
        functools.partial(project_kernel, n),
        out_shape=(
            jax.ShapeDtypeStruct((ways, toks, width), jnp.bfloat16),
            jax.ShapeDtypeStruct((ways, n, rows, width), jnp.bfloat16),
        ),
        in_specs=[VMEM, VMEM],
        out_specs=(VMEM, VMEM),
        scratch_shapes=[
            pltpu.VMEM((ways, toks, width), jnp.float32),
            pltpu.SemaphoreType.DMA,
            pltpu.SemaphoreType.DMA((2, n - 1)),
            pltpu.SemaphoreType.DMA((2, n - 1)),
        ],
        compiler_params=pltpu.CompilerParams(
            collective_id=0, has_side_effects=True, vmem_limit_bytes=56 << 20
        ),
        cost_estimate=pl.CostEstimate(
            flops=2 * toks * n * rows * ways * width, bytes_accessed=1 << 24, transcendentals=0
        ),
    )(tokens, weights)


def scan_kernel(n, sign, x_ref, out_ref, total, send_buf, recv_buf, send_sem, recv_sem):
    me = lax.axis_index("seq")
    steps = [1 << b for b in range((n - 1).bit_length())]
    barrier = pltpu.get_barrier_semaphore()
    for far in steps:
        source = lax.rem(me - sign * far + n, n)
        pl.semaphore_signal(barrier, inc=1, device_id={"seq": source}, device_id_type=MESH)
    pl.semaphore_wait(barrier, len(steps))
    total[...] = x_ref[...]
    out_ref[...] = jnp.zeros_like(out_ref)
    rank = me if sign == 1 else n - 1 - me
    for place, far in enumerate(steps):
        send_buf[place] = total[...].astype(jnp.bfloat16)
        copy = pltpu.make_async_remote_copy(
            src_ref=send_buf.at[place],
            dst_ref=recv_buf.at[place],
            send_sem=send_sem.at[place],
            recv_sem=recv_sem.at[place],
            device_id={"seq": lax.rem(me + sign * far + n, n)},
            device_id_type=MESH,
        )
        copy.start()
        copy.wait()
        keep = jnp.broadcast_to(rank >= far, out_ref.shape)
        got = jnp.where(keep, recv_buf[place].astype(jnp.float32), 0.0)
        total[...] += got
        out_ref[...] += got


def carried(states, totals, n, sign):
    heads, features, size = states.shape
    flat_totals = totals.reshape(-1, size)
    used = flat_totals.shape[0]
    pad = (-(used)) % 16
    packed = jnp.concatenate(
        [states.reshape(-1, size), flat_totals, jnp.zeros((pad, size), jnp.float32)], 0
    )
    steps = (n - 1).bit_length()
    out = pl.pallas_call(
        functools.partial(scan_kernel, n, sign),
        out_shape=jax.ShapeDtypeStruct(packed.shape, jnp.float32),
        in_specs=[VMEM],
        out_specs=VMEM,
        scratch_shapes=[
            pltpu.VMEM(packed.shape, jnp.float32),
            pltpu.VMEM((steps,) + packed.shape, jnp.bfloat16),
            pltpu.VMEM((steps,) + packed.shape, jnp.bfloat16),
            pltpu.SemaphoreType.DMA((steps,)),
            pltpu.SemaphoreType.DMA((steps,)),
        ],
        compiler_params=pltpu.CompilerParams(
            collective_id=1 if sign == 1 else 2,
            has_side_effects=True,
            vmem_limit_bytes=32 << 20,
        ),
    )(packed)
    split = heads * features
    return out[:split].reshape(states.shape), out[split : split + used].reshape(totals.shape)


def grads_kernel(
    n, groups, tok_ref, grad_ref, full_ref, input_ref, weight_ref,
    ring, part_out, part_in, send_sem, recv_sem, part_send, part_recv,
):
    me = lax.axis_index("seq")
    group = lax.axis_index("head")
    place = ring_pos(me, n)
    ahead, behind = ring_index(place + 1, n), ring_index(place - 1, n)
    rows = full_ref.shape[2]
    others = tuple({"head": lax.rem(group + k, groups)} for k in range(1, groups))
    greet_ring(ahead, behind, others)

    def term(way, step):
        owner = ring_index(place - 1 - step if way == 0 else place + 1 + step, n)
        columns = pl.ds(pl.multiple_of(owner * rows, rows), rows)
        return lax.dot_general(
            tok_ref[:, columns],
            grad_ref[way],
            (((0,), (0,)), ((), ())),
            preferred_element_type=jnp.float32,
        )

    def ring_copy(way, step):
        return pltpu.make_async_remote_copy(
            src_ref=ring.at[way, step],
            dst_ref=ring.at[way, step + 1],
            send_sem=send_sem.at[way, step],
            recv_sem=recv_sem.at[way, step],
            device_id={"seq": ahead if way == 0 else behind},
            device_id_type=MESH,
        )

    for way in range(2):
        ring[way, 0] = term(way, 0).astype(jnp.bfloat16)
        ring_copy(way, 0).start()

    def part_copy(k):
        return pltpu.make_async_remote_copy(
            src_ref=part_out.at[k],
            dst_ref=part_in.at[k],
            send_sem=part_send.at[k],
            recv_sem=part_recv.at[k],
            device_id={"head": lax.rem(group + k + 1, groups)},
            device_id_type=MESH,
        )

    blocks = n // groups

    def one_part(k, carry):
        first = lax.rem(group + k + 1, groups) * blocks

        def one_block(c, carry):
            piece = None
            for way in range(2):
                product = lax.dot_general(
                    grad_ref[way],
                    full_ref[way, first + c],
                    (((1,), (1,)), ((), ())),
                    preferred_element_type=jnp.float32,
                )
                piece = product if piece is None else piece + product
            columns = pl.ds(pl.multiple_of(c * rows, rows), rows)
            part_out[k, :, columns] = piece.astype(jnp.bfloat16)
            return carry

        lax.fori_loop(0, blocks, one_block, 0)

        @pl.when(k < groups - 1)
        def _():
            part_copy(k).start()

        return carry

    lax.fori_loop(0, groups, one_part, 0)

    def one(step, carry):
        for way in range(2):
            own = term(way, step)
            ring_copy(way, step - 1).wait()
            ring[way, step] = (ring[way, step].astype(jnp.float32) + own).astype(jnp.bfloat16)
            ring_copy(way, step).start()
        return carry

    lax.fori_loop(1, n - 1, one, 0)
    total = part_out[groups - 1].astype(jnp.float32)
    for k in range(groups - 1):
        part_copy(k).wait()
        total += part_in[k].astype(jnp.float32)
    input_ref[...] = total.astype(input_ref.dtype)
    for way in range(2):
        own = term(way, n - 1)
        ring_copy(way, n - 2).wait()
        weight_ref[way] = ring[way, n - 1].astype(jnp.float32) + own


def gradients(tokens, grads, full, n, groups):
    ways, _, rows, width = full.shape
    toks, model = tokens.shape
    share = model // groups
    return pl.pallas_call(
        functools.partial(grads_kernel, n, groups),
        out_shape=(
            jax.ShapeDtypeStruct((toks, share), jnp.bfloat16),
            jax.ShapeDtypeStruct((ways, rows, width), jnp.float32),
        ),
        in_specs=[VMEM, VMEM, VMEM],
        out_specs=(VMEM, VMEM),
        scratch_shapes=[
            pltpu.VMEM((ways, n, rows, width), jnp.bfloat16),
            pltpu.VMEM((groups, toks, share), jnp.bfloat16),
            pltpu.VMEM((groups - 1, toks, share), jnp.bfloat16),
            pltpu.SemaphoreType.DMA((2, n - 1)),
            pltpu.SemaphoreType.DMA((2, n - 1)),
            pltpu.SemaphoreType.DMA((groups - 1,)),
            pltpu.SemaphoreType.DMA((groups - 1,)),
        ],
        compiler_params=pltpu.CompilerParams(
            collective_id=3, has_side_effects=True, vmem_limit_bytes=58 << 20
        ),
    )(tokens, grads, full)


def two_ways(a):
    return a.reshape(a.shape[0], 2, -1).transpose(1, 0, 2)


def feature_map(act, seed, scaled):
    factor = seed_step * act.shape[-1] ** (-0.25)
    projected = ein("htd,hdm->htm", act, seed) * factor
    return jnp.exp(projected - 0.5 * jnp.sum(scaled * scaled, -1, keepdims=True)) / math.sqrt(
        seed.shape[-1]
    )


def feature_grad(upstream, features, scaled, seed):
    weighted = upstream * features
    projected = ein("htm,hdm->htd", weighted, seed) * seed_step
    return (projected - jnp.sum(weighted, -1, keepdims=True) * scaled) * scaled.shape[-1] ** (-0.25)


def head_major(value_matrix, heads_here):
    tok_rows = value_matrix.shape[0]
    return value_matrix.astype(jnp.float32).reshape(tok_rows, heads_here, -1).transpose(1, 0, 2)


def token_major(value_matrix):
    return value_matrix.transpose(1, 0, 2).reshape(value_matrix.shape[1], -1).astype(jnp.bfloat16)


def per_device(n, groups, tokens, w_query, w_key, w_value, omega_seed, grad_out):
    heads_here = omega_seed.shape[0]
    head_size = omega_seed.shape[1]
    weights = two_ways(jnp.concatenate([w_query, w_key, w_value], 1))
    activations, full = project(tokens, weights, n)
    both = activations.transpose(1, 0, 2).reshape(tokens.shape[0], -1)
    query_act, key_act, value_act = jnp.split(both, 3, 1)
    scale_in = head_size ** (-0.25)
    query_rows = head_major(query_act, heads_here)
    query_scaled = query_rows * scale_in
    key_rows = head_major(key_act, heads_here)
    key_scaled = key_rows * scale_in
    value_matrix = head_major(value_act, heads_here)
    upstream = head_major(grad_out, heads_here)
    query_feature_rows = feature_map(query_rows, omega_seed, query_scaled)
    source_embedding_entries = feature_map(key_rows, omega_seed, key_scaled)
    tok_rows = tokens.shape[0]
    causal = jnp.tril(jnp.ones((tok_rows, tok_rows), jnp.float32))
    block_local_states = ein(
        "vzn,vza->vna", source_embedding_entries, value_matrix
    )
    local_totals = jnp.sum(source_embedding_entries, 1)
    prefix_carried_outer, prefix_normaliser_accrual = carried(
        block_local_states, local_totals, n, 1
    )
    attention_scores = (
        ein(
            "htm,hsm->hts",
            query_feature_rows,
            source_embedding_entries
        )
        * causal
    )
    attention_numerator = ein(
        "xyw,xwc->xyc", attention_scores, value_matrix
    ) + ein(
        "sji,six->sjx", query_feature_rows, prefix_carried_outer
    )
    normer = jnp.sum(attention_scores, -1) + ein(
        "htm,hm->ht", query_feature_rows, prefix_normaliser_accrual
    )
    output = attention_numerator / normer[..., None]
    dividend_cotangent = upstream / normer[..., None]
    normaliser_cotangent = -jnp.sum(upstream * output, -1) / normer
    couplewise_products = (
        ein(
            "htd,hsd->hts", dividend_cotangent, value_matrix
        )
        + normaliser_cotangent[..., None]
    ) * causal
    target_embedding_cotangent = (
        ein(
            "mez,mzo->meo",
            couplewise_products,
            source_embedding_entries
        )
        + ein(
            "zrc,zfc->zrf",
            dividend_cotangent,
            prefix_carried_outer
        )
        + normaliser_cotangent[..., None] * prefix_normaliser_accrual[:, None, :]
    )
    query16 = token_major(
        feature_grad(target_embedding_cotangent, query_feature_rows, query_scaled, omega_seed)
    )
    subsequent_local_states = ein(
        "opu,opc->ouc", query_feature_rows, dividend_cotangent
    )
    later_totals = ein(
        "htm,ht->hm", query_feature_rows, normaliser_cotangent
    )
    subsequent_states, subsequent_sum = carried(
        subsequent_local_states, later_totals, n, -1
    )
    key_feature_gradient = (
        ein(
            "ykl,yku->ylu", couplewise_products, query_feature_rows
        )
        + ein(
            "bgq,bxq->bgx", value_matrix, subsequent_states
        )
        + subsequent_sum[:, None, :]
    )
    value_gradient_rows = ein(
        "vkm,vky->vmy", attention_scores, dividend_cotangent
    ) + ein(
        "tjr,tro->tjo", source_embedding_entries, subsequent_states
    )
    key16 = token_major(
        feature_grad(key_feature_gradient, source_embedding_entries, key_scaled, omega_seed)
    )
    value16 = token_major(value_gradient_rows)
    joined = jnp.concatenate([query16, key16, value16], 1)
    input_grad, weight_total = gradients(tokens, two_ways(joined), full, n, groups)
    weight_total = weight_total.transpose(1, 0, 2).reshape(w_query.shape[0], -1)
    columns = query16.shape[1]
    query_wgrad = weight_total[:, :columns]
    key_wgrad = weight_total[:, columns : 2 * columns]
    value_wgrad = weight_total[:, 2 * columns :]
    return (input_grad, query_wgrad, key_wgrad, value_wgrad)


def solution(mesh):
    placed = (
        P("seq", None),
        P("seq", "head"),
        P("seq", "head"),
        P("seq", "head"),
        P("head", None, None),
        P("seq", "head"),
    )
    return jax.shard_map(
        functools.partial(per_device, mesh.shape["seq"], mesh.shape["head"]),
        mesh=mesh,
        in_specs=placed,
        out_specs=(P("seq", "head"), P("seq", "head"), P("seq", "head"), P("seq", "head")),
        check_vma=False,
    )
```

time: 660 us -> 369 us (0.56); the launches traced: 653 us -> 369 us
  waiting for transfers between devices: 445 us -> 0 us
  Pallas kernels: 0 us -> 321 us
  matrix products: 101 us -> 17.3 us
  blocking collectives: 72.5 us -> 0 us
  local copies, waits for them, and re-layouts: 10.3 us -> 26.4 us
  between operations: 15.1 us -> 1.08 us
    pallas_call x0 -> x4, Pallas kernels: none -> 321 us  [the longest x1 135 us: gradients(): pl.pallas_call(functools.partial(grads_kernel, n, groups), out_shape=(jax...]
    reduce_scatter x2 -> x0, waiting for transfers between devices: 228 us -> none  [the longest x1 187 us: per_device(): lax.psum_scatter(projection_term(tokens, joined).astype(jnp.bfloat16), 's...]
    all_gather x5 -> x0, waiting for transfers between devices: 215 us -> none  [the longest x1 76.8 us: per_device(): lax.all_gather(w_value, 'seq', axis=0, tiled=True)]
    dot_general x25 -> x18, matrix products: 101 us -> 17.3 us  [ein(): jnp.einsum(spec, a.astype(jnp.bfloat16), b.astype(jnp.bfloat16), preferre...]
    all_gather x2 -> x0, blocking collectives: 72.5 us -> none  [the longest x1 45.9 us: carried_in_2(): lax.all_gather(a.astype(kind), axis)]
    add x14 -> x0, other arithmetic: 7.58 us -> none  [add_states(): return (earlier[0] + later_part[0], earlier[1] + later_part[1])]
  transfers between devices with their start and end apart: 7 -> 0, of which waited for: 6 -> 0; matrix products, arithmetic and copies ran while one was open for 12% -> 0% of each run, Pallas kernels for 0% -> 0%
where the time goes in v1:
time: 369 us
  Pallas kernels  321 us (87%)
  local copies, waits for them, and re-layouts  26.4 us (7%)
  matrix products  17.3 us (5%)
    pallas_call x1, Pallas kernels, gradients(): pl.pallas_call(functools.partial(grads_kernel, n, groups), out_shape=(jax...  135 us
    pallas_call x1, Pallas kernels, project(): pl.pallas_call(functools.partial(project_kernel, n), out_shape=(jax.Shape...  134 us
    pallas_call x2, Pallas kernels, carried(): pl.pallas_call(functools.partial(scan_kernel, n, sign), out_shape=jax.Sha...  51.8 us
    dot_general x18, matrix products, ein(): jnp.einsum(spec, a.astype(jnp.bfloat16), b.astype(jnp.bfloat16), preferre...  17.3 us
    unnamed x51, local copies, waits for them, and re-layouts  9.85 us

profile of v1, /device:TPU:0, one launch (start us, length us, event | category | flops | bytes accessed | tf_op | source)
XLA Modules:
  0.0 368.8 jit_solution(9322081495276211328)
XLA Ops:
  0.7 1.2 convert_element_type.100
  1.9 1.3 copy.33
  3.9 1.6 copy.36
  5.6 1.2 copy.32
  6.8 133.7 %shard_map.93 = (bf16[2,512,768]{2,1,0:T(8,128)(2,1)}, bf16[2,8,512,768]{3,2,1,0:T(8,128)(2,1)}) custom-call(bf16[512,4096]{1,0:T(8,128)(2,1)} %tok_ref.3, bf16[2,512,768]{2,1,0:T(8,128)(2,1)} %bitcast.126), custom_call_target="tpu_custom_call" | custom-call | flops 6442450944 | bytes 16777216 | tf_op jit(solution)/shard_map/pallas_call | solution.py:97
  140.4 1.9 copy.37
  144.7 1.3 copy.38
  147.1 2.0 fusion.34
  149.0 2.1 fusion.32
  151.1 1.5 fusion.21
  152.8 26.2 %shard_map.94 = f32[1040,128]{1,0:T(8,128)S(1)} custom-call(f32[1040,128]{1,0:T(8,128)S(1)} %maximum_maximum_fusion.x_ref), custom_call_target="tpu_custom_call" | custom-call | tf_op jit(solution)/shard_map/pallas_call | solution.py:158
  180.7 1.2 fusion.38
  182.5 1.8 fusion.25
  185.1 1.3 maximum_maximum_fusion.1.x_ref
  186.4 25.6 %shard_map.95 = f32[1040,128]{1,0:T(8,128)S(1)} custom-call(f32[1040,128]{1,0:T(8,128)S(1)} %maximum_maximum_fusion.1.x_ref), custom_call_target="tpu_custom_call" | custom-call | tf_op jit(solution)/shard_map/pallas_call | solution.py:158
  212.1 1.1 fusion.8
  213.2 1.9 multiply_convert_fusion
  221.5 1.6 copy.60
  223.0 135.1 %shard_map.96 = (bf16[512,1024]{1,0:T(8,128)(2,1)}, f32[2,512,768]{2,1,0:T(8,128)}) custom-call(bf16[512,4096]{1,0:T(8,128)(2,1)} %tok_ref.3, bf16[2,512,768]{2,1,0:T(8,128)(2,1)} %bitcast.110, bf16[2,8,512,768]{3,2,1,0:T(8,128)(2,1)} %get-tuple-element.9.full_ref), custom_call_target="tpu_custom_call" | custom-call | tf_op jit(solution)/shard_map/pallas_call | solution.py:279
  358.2 3.5 copy.61
  361.7 2.2 fusion.31
  363.9 1.3 copy.64
  365.2 1.3 copy.63
  366.5 1.3 copy.62
  (84 shorter events, 14.5 us)
Async XLA Ops:
  0.6 2.9 copy-start.21
  0.6 2.6 copy-start.20
  1.9 147.1 %copy-start.9 = (bf16[4,128,256]{2,1,0:T(8,128)(2,1)}, bf16[4,128,256]{2,1,0:T(8,128)(2,1)S(1)}, u32[]{:S(2)}) copy-start(bf16[4,128,256]{2,1,0:T(8,128)(2,1)S(1)} %convert_element_type.100) | copy-start | bytes 786436
  3.9 1.7 copy-start.19
  143.7 5.3 %copy-start.5 = (bf16[512,512]{0,1:T(8,128)(2,1)}, bf16[512,512]{0,1:T(8,128)(2,1)S(1)}, u32[]{:S(2)}) copy-start(bf16[512,512]{0,1:T(8,128)(2,1)S(1)} %get-tuple-element.25) | copy-start | bytes 1572868
  143.7 2.3 copy-start.12
  147.1 2.0 copy-start.11
  179.0 5.3 %copy-start.16 = (bf16[1024,128]{1,0:T(8,128)(2,1)}, bf16[1024,128]{1,0:T(8,128)(2,1)S(1)}, u32[]{:S(2)}) copy-start(bf16[1024,128]{1,0:T(8,128)(2,1)S(1)} %slice.38) | copy-start | bytes 786436
  179.3 1.2 copy-start.7
  180.1 1.8 copy-start.6
  180.7 1.8 copy-start
  185.1 27.0 %copy-start.8 = (f32[4,512,128]{1,2,0:T(8,128)S(1)}, f32[4,512,128]{1,2,0:T(8,128)}, u32[]{:S(2)}) copy-start(f32[4,512,128]{1,2,0:T(8,128)} %fusion.25) | copy-start | bytes 3145732
  215.1 1.6 copy-start.2
  215.1 1.7 copy-start.4
  217.4 1.0 copy-start.1
  217.4 1.8 copy-start.3
  217.4 1.8 copy-start.17
  219.1 1.0 copy-start.10
  219.1 1.1 copy-start.14
  219.8 1.1 copy-start.13
  220.3 1.1 copy-start.15
  365.2 2.6 copy-start.18

commit v2 on v1

--- a/solution.py
+++ b/solution.py
@@ -43,19 +43,57 @@
     pl.semaphore_wait(barrier, 2 + len(others))
 
 
-def project_kernel(n, tok_ref, w_ref, act_ref, full_ref, acc, local_sem, send_sem, recv_sem):
+def pieces_of(rows):
+    half = rows // 2
+    return tuple((part, pl.ds(part * half, half)) for part in range(2))
+
+
+def split_columns(cols):
+    half = cols // 2
+    return (
+        (0, slice(0, cols), 0, slice(0, cols)),
+        (1, slice(0, half), 0, slice(cols, cols + half)),
+        (1, slice(half, cols), 1, slice(0, half)),
+        (2, slice(0, cols), 1, slice(half, half + cols)),
+    )
+
+
+def project_kernel(
+    n, tok_ref, wq_ref, wk_ref, wv_ref, q_ref, k_ref, v_ref, full_ref, acc, send_sem, recv_sem
+):
     me = lax.axis_index("seq")
     place = ring_pos(me, n)
     ahead, behind = ring_index(place + 1, n), ring_index(place - 1, n)
-    rows = w_ref.shape[1]
+    rows, cols = wq_ref.shape
     greet_ring(ahead, behind, ())
-    own = pltpu.make_async_copy(w_ref, full_ref.at[:, me], local_sem)
-    own.start()
-    acc[...] = jnp.zeros_like(acc)
-    own.wait()
+    sources = (wq_ref, wk_ref, wv_ref)
+    for matrix, columns, way, target in split_columns(cols):
+        full_ref[way, me, :, target] = sources[matrix][:, columns]
 
     def owner_of(way, step):
         return ring_index(place - step if way == 0 else place + step, n)
+
+    def ring_copy(way, step, part, span):
+        owner = owner_of(way, step)
+        return pltpu.make_async_remote_copy(
+            src_ref=full_ref.at[way, owner, span],
+            dst_ref=full_ref.at[way, owner, span],
+            send_sem=send_sem.at[way, step, part],
+            recv_sem=recv_sem.at[way, step, part],
+            device_id={"seq": ahead if way == 0 else behind},
+            device_id_type=MESH,
+        )
+
+    def arrival(way, step, part, span):
+        owner = owner_of(way, step + 1)
+        return pltpu.make_async_remote_copy(
+            src_ref=full_ref.at[way, owner, span],
+            dst_ref=full_ref.at[way, owner, span],
+            send_sem=send_sem.at[way, step, part],
+            recv_sem=recv_sem.at[way, step, part],
+            device_id={"seq": ahead if way == 0 else behind},
+            device_id_type=MESH,
+        )
 
     def multiply(step):
         for way in range(2):
@@ -65,56 +103,60 @@
                 tok_ref[:, columns], full_ref[way, owner], preferred_element_type=jnp.float32
             )
 
+    for part, span in pieces_of(rows):
+        for way in range(2):
+            ring_copy(way, 0, part, span).start()
+    acc[...] = jnp.zeros_like(acc)
+    multiply(0)
+
     def one(step, carry):
-        copies = []
-        for way, target in ((0, ahead), (1, behind)):
-            owner = owner_of(way, step)
-            copies.append(
-                pltpu.make_async_remote_copy(
-                    src_ref=full_ref.at[way, owner],
-                    dst_ref=full_ref.at[way, owner],
-                    send_sem=send_sem.at[way, step],
-                    recv_sem=recv_sem.at[way, step],
-                    device_id={"seq": target},
-                    device_id_type=MESH,
-                )
-            )
-        for copy in copies:
-            copy.start()
+        for part, span in pieces_of(rows):
+            for way in range(2):
+                arrival(way, step - 1, part, span).wait_recv()
+                ring_copy(way, step, part, span).start()
         multiply(step)
-        for copy in copies:
-            copy.wait()
         return carry
 
-    lax.fori_loop(0, n - 1, one, 0)
+    lax.fori_loop(1, n - 1, one, 0)
+    for part, span in pieces_of(rows):
+        for way in range(2):
+            arrival(way, n - 2, part, span).wait_recv()
     multiply(n - 1)
-    act_ref[...] = acc[...].astype(act_ref.dtype)
-
-
-def project(tokens, weights, n):
-    ways, rows, width = weights.shape
+    results = (q_ref, k_ref, v_ref)
+    for matrix, columns, way, source in split_columns(cols):
+        results[matrix][:, columns] = acc[way, :, source].astype(jnp.bfloat16)
+
+    def sent(step, carry):
+        for part, span in pieces_of(rows):
+            for way in range(2):
+                ring_copy(way, step, part, span).wait_send()
+        return carry
+
+    lax.fori_loop(0, n - 1, sent, 0)
+
+
+def project(tokens, w_query, w_key, w_value, n):
+    rows, cols = w_query.shape
+    width = 3 * cols // 2
     toks = tokens.shape[0]
+    act = jax.ShapeDtypeStruct((toks, cols), jnp.bfloat16)
     return pl.pallas_call(
         functools.partial(project_kernel, n),
-        out_shape=(
-            jax.ShapeDtypeStruct((ways, toks, width), jnp.bfloat16),
-            jax.ShapeDtypeStruct((ways, n, rows, width), jnp.bfloat16),
-        ),
-        in_specs=[VMEM, VMEM],
-        out_specs=(VMEM, VMEM),
+        out_shape=(act, act, act, jax.ShapeDtypeStruct((2, n, rows, width), jnp.bfloat16)),
+        in_specs=[VMEM] * 4,
+        out_specs=(VMEM,) * 4,
         scratch_shapes=[
-            pltpu.VMEM((ways, toks, width), jnp.float32),
-            pltpu.SemaphoreType.DMA,
-            pltpu.SemaphoreType.DMA((2, n - 1)),
-            pltpu.SemaphoreType.DMA((2, n - 1)),
+            pltpu.VMEM((2, toks, width), jnp.float32),
+            pltpu.SemaphoreType.DMA((2, n - 1, 2)),
+            pltpu.SemaphoreType.DMA((2, n - 1, 2)),
         ],
         compiler_params=pltpu.CompilerParams(
             collective_id=0, has_side_effects=True, vmem_limit_bytes=56 << 20
         ),
         cost_estimate=pl.CostEstimate(
-            flops=2 * toks * n * rows * ways * width, bytes_accessed=1 << 24, transcendentals=0
+            flops=4 * toks * n * rows * width, bytes_accessed=1 << 24, transcendentals=0
         ),
-    )(tokens, weights)
+    )(tokens, w_query, w_key, w_value)
 
 
 def scan_kernel(n, sign, x_ref, out_ref, total, send_buf, recv_buf, send_sem, recv_sem):
@@ -178,40 +220,40 @@
 
 
 def grads_kernel(
-    n, groups, tok_ref, grad_ref, full_ref, input_ref, weight_ref,
-    ring, part_out, part_in, send_sem, recv_sem, part_send, part_recv,
+    n, groups, tok_ref, q_ref, k_ref, v_ref, full_ref, input_ref, wq_ref, wk_ref, wv_ref,
+    grad_ref, ring, own, part_out, part_in, send_sem, recv_sem, part_send, part_recv,
 ):
     me = lax.axis_index("seq")
     group = lax.axis_index("head")
     place = ring_pos(me, n)
     ahead, behind = ring_index(place + 1, n), ring_index(place - 1, n)
     rows = full_ref.shape[2]
+    cols = q_ref.shape[1]
     others = tuple({"head": lax.rem(group + k, groups)} for k in range(1, groups))
     greet_ring(ahead, behind, others)
+    sources = (q_ref, k_ref, v_ref)
+    for matrix, columns, way, target in split_columns(cols):
+        grad_ref[way, :, target] = sources[matrix][:, columns]
 
     def term(way, step):
         owner = ring_index(place - 1 - step if way == 0 else place + 1 + step, n)
         columns = pl.ds(pl.multiple_of(owner * rows, rows), rows)
-        return lax.dot_general(
+        own[way] = lax.dot_general(
             tok_ref[:, columns],
             grad_ref[way],
             (((0,), (0,)), ((), ())),
             preferred_element_type=jnp.float32,
         )
 
-    def ring_copy(way, step):
+    def ring_copy(way, step, part, span):
         return pltpu.make_async_remote_copy(
-            src_ref=ring.at[way, step],
-            dst_ref=ring.at[way, step + 1],
-            send_sem=send_sem.at[way, step],
-            recv_sem=recv_sem.at[way, step],
+            src_ref=ring.at[way, step, span],
+            dst_ref=ring.at[way, step + 1, span],
+            send_sem=send_sem.at[way, step, part],
+            recv_sem=recv_sem.at[way, step, part],
             device_id={"seq": ahead if way == 0 else behind},
             device_id_type=MESH,
         )
-
-    for way in range(2):
-        ring[way, 0] = term(way, 0).astype(jnp.bfloat16)
-        ring_copy(way, 0).start()
 
     def part_copy(k):
         return pltpu.make_async_remote_copy(
@@ -250,57 +292,81 @@
 
         return carry
 
-    lax.fori_loop(0, groups, one_part, 0)
+    for way in range(2):
+        term(way, 0)
+        for part, span in pieces_of(rows):
+            ring[way, 0, span] = own[way, span].astype(jnp.bfloat16)
+            ring_copy(way, 0, part, span).start()
+    for way in range(2):
+        term(way, 1)
 
     def one(step, carry):
+        @pl.when(step <= groups)
+        def _():
+            one_part(step - 1, 0)
+
+        for part, span in pieces_of(rows):
+            for way in range(2):
+                ring_copy(way, step - 1, part, span).wait_recv()
+                ring[way, step, span] = (
+                    ring[way, step, span].astype(jnp.float32) + own[way, span]
+                ).astype(jnp.bfloat16)
+                ring_copy(way, step, part, span).start()
         for way in range(2):
-            own = term(way, step)
-            ring_copy(way, step - 1).wait()
-            ring[way, step] = (ring[way, step].astype(jnp.float32) + own).astype(jnp.bfloat16)
-            ring_copy(way, step).start()
+            term(way, step + 1)
         return carry
 
     lax.fori_loop(1, n - 1, one, 0)
+    if groups > n - 2:
+        lax.fori_loop(n - 2, groups, one_part, 0)
     total = part_out[groups - 1].astype(jnp.float32)
     for k in range(groups - 1):
         part_copy(k).wait()
         total += part_in[k].astype(jnp.float32)
     input_ref[...] = total.astype(input_ref.dtype)
-    for way in range(2):
-        own = term(way, n - 1)
-        ring_copy(way, n - 2).wait()
-        weight_ref[way] = ring[way, n - 1].astype(jnp.float32) + own
-
-
-def gradients(tokens, grads, full, n, groups):
+    for part, span in pieces_of(rows):
+        for way in range(2):
+            ring_copy(way, n - 2, part, span).wait_recv()
+    results = (wq_ref, wk_ref, wv_ref)
+    for matrix, columns, way, source in split_columns(cols):
+        results[matrix][:, columns] = (
+            ring[way, n - 1, :, source].astype(jnp.float32) + own[way, :, source]
+        )
+
+    def sent(step, carry):
+        for part, span in pieces_of(rows):
+            for way in range(2):
+                ring_copy(way, step, part, span).wait_send()
+        return carry
+
+    lax.fori_loop(0, n - 1, sent, 0)
+
+
+def gradients(tokens, query16, key16, value16, full, n, groups):
     ways, _, rows, width = full.shape
     toks, model = tokens.shape
     share = model // groups
+    wgrad = jax.ShapeDtypeStruct((rows, query16.shape[1]), jnp.float32)
     return pl.pallas_call(
         functools.partial(grads_kernel, n, groups),
-        out_shape=(
-            jax.ShapeDtypeStruct((toks, share), jnp.bfloat16),
-            jax.ShapeDtypeStruct((ways, rows, width), jnp.float32),
-        ),
-        in_specs=[VMEM, VMEM, VMEM],
-        out_specs=(VMEM, VMEM),
+        out_shape=(jax.ShapeDtypeStruct((toks, share), jnp.bfloat16), wgrad, wgrad, wgrad),
+        in_specs=[VMEM] * 5,
+        out_specs=(VMEM,) * 4,
         scratch_shapes=[
+            pltpu.VMEM((ways, toks, width), jnp.bfloat16),
             pltpu.VMEM((ways, n, rows, width), jnp.bfloat16),
+            pltpu.VMEM((ways, rows, width), jnp.float32),
             pltpu.VMEM((groups, toks, share), jnp.bfloat16),
             pltpu.VMEM((groups - 1, toks, share), jnp.bfloat16),
-            pltpu.SemaphoreType.DMA((2, n - 1)),
-            pltpu.SemaphoreType.DMA((2, n - 1)),
+            pltpu.SemaphoreType.DMA((2, n - 1, 2)),
+            pltpu.SemaphoreType.DMA((2, n - 1, 2)),
             pltpu.SemaphoreType.DMA((groups - 1,)),
             pltpu.SemaphoreType.DMA((groups - 1,)),
         ],
         compiler_params=pltpu.CompilerParams(
-            collective_id=3, has_side_effects=True, vmem_limit_bytes=58 << 20
+            collective_id=3, has_side_effects=True, vmem_limit_bytes=60 << 20
         ),
-    )(tokens, grads, full)
-
-
-def two_ways(a):
-    return a.reshape(a.shape[0], 2, -1).transpose(1, 0, 2)
+    )(tokens, query16, key16, value16, full)
 
 
 def feature_map(act, seed, scaled):
@@ -329,10 +395,7 @@
 def per_device(n, groups, tokens, w_query, w_key, w_value, omega_seed, grad_out):
     heads_here = omega_seed.shape[0]
     head_size = omega_seed.shape[1]
-    weights = two_ways(jnp.concatenate([w_query, w_key, w_value], 1))
-    activations, full = project(tokens, weights, n)
-    both = activations.transpose(1, 0, 2).reshape(tokens.shape[0], -1)
-    query_act, key_act, value_act = jnp.split(both, 3, 1)
+    query_act, key_act, value_act, full = project(tokens, w_query, w_key, w_value, n)
     scale_in = head_size ** (-0.25)
     query_rows = head_major(query_act, heads_here)
     query_scaled = query_rows * scale_in
@@ -419,13 +482,9 @@
         feature_grad(key_feature_gradient, source_embedding_entries, key_scaled, omega_seed)
     )
     value16 = token_major(value_gradient_rows)
-    joined = jnp.concatenate([query16, key16, value16], 1)
-    input_grad, weight_total = gradients(tokens, two_ways(joined), full, n, groups)
-    weight_total = weight_total.transpose(1, 0, 2).reshape(w_query.shape[0], -1)
-    columns = query16.shape[1]
-    query_wgrad = weight_total[:, :columns]
-    key_wgrad = weight_total[:, columns : 2 * columns]
-    value_wgrad = weight_total[:, 2 * columns :]
+    input_grad, query_wgrad, key_wgrad, value_wgrad = gradients(
+        tokens, query16, key16, value16, full, n, groups
+    )
     return (input_grad, query_wgrad, key_wgrad, value_wgrad)
 
 

time: 369 us -> 357 us (0.967)
  local copies, waits for them, and re-layouts: 26.4 us -> 16.8 us
    transpose x2 -> x0, local copies, waits for them, and re-layouts: 5.42 us -> none  [the longest x1 3.52 us: per_device(): weight_total = weight_total.transpose(1, 0, 2).reshape(w_query.shape[0], -1)]
    pallas_call x1, Pallas kernels: 135 us -> 131 us  [gradients(): pl.pallas_call(functools.partial(grads_kernel, n, groups), out_shape=(jax...]
    unnamed x51 -> x48, local copies, waits for them, and re-layouts: 9.85 us -> 8.81 us
where the time goes in v2:
time: 357 us; the launch traced here: 356 us
  Pallas kernels  318 us (89%)
  matrix products  17.2 us (5%)
  local copies, waits for them, and re-layouts  16.8 us (5%)
    pallas_call x1, Pallas kernels, project(): pl.pallas_call(functools.partial(project_kernel, n), out_shape=(act, act,...  132 us
    pallas_call x1, Pallas kernels, gradients(): pl.pallas_call(functools.partial(grads_kernel, n, groups), out_shape=(jax...  131 us
    pallas_call x2, Pallas kernels, carried(): pl.pallas_call(functools.partial(scan_kernel, n, sign), out_shape=jax.Sha...  54.8 us
    dot_general x18, matrix products, ein(): jnp.einsum(spec, a.astype(jnp.bfloat16), b.astype(jnp.bfloat16), preferre...  17.2 us
    unnamed x48, local copies, waits for them, and re-layouts  8.81 us

profile of v2, /device:TPU:0, one launch (start us, length us, event | category | flops | bytes accessed | tf_op | source)
XLA Modules:
  0.0 356.3 jit_solution(10141024974811257215)
XLA Ops:
  0.7 1.1 convert_element_type.96
  2.0 1.2 copy.10
  3.2 132.3 %shard_map.93 = (bf16[512,512]{1,0:T(8,128)(2,1)}, bf16[512,512]{1,0:T(8,128)(2,1)}, bf16[512,512]{1,0:T(8,128)(2,1)}, bf16[2,8,512,768]{3,2,1,0:T(8,128)(2,1)}) custom-call(bf16[512,4096]{1,0:T(8,128)(2,1)} %tok_ref.3, bf16[512,512]{1,0:T(8,128)(2,1)} %wq_ref.1, bf16[512,512]{1,0:T(8,128)(2,1)} %wk_ref.1, bf16[512,512]{1,0:T(8,128)(2,1)} %wv_ref.1), custom_call_target="tpu_custom_call" | custom-call | flops 6442450944 | bytes 16777216 | tf_op jit(solution)/shard_map/pallas_call | solution.py:143
  135.4 1.3 copy.99
  137.6 1.3 copy.100
  139.0 2.0 fusion.33
  141.0 2.1 fusion.32
  143.1 1.5 fusion.21
  144.8 27.2 %shard_map.94 = f32[1040,128]{1,0:T(8,128)S(1)} custom-call(f32[1040,128]{1,0:T(8,128)S(1)} %maximum_maximum_fusion.x_ref), custom_call_target="tpu_custom_call" | custom-call | tf_op jit(solution)/shard_map/pallas_call | solution.py:200
  173.7 1.2 fusion.37
  174.9 1.8 fusion.27
  178.1 1.3 maximum_maximum_fusion.1.x_ref
  179.4 27.5 %shard_map.95 = f32[1040,128]{1,0:T(8,128)S(1)} custom-call(f32[1040,128]{1,0:T(8,128)S(1)} %maximum_maximum_fusion.1.x_ref), custom_call_target="tpu_custom_call" | custom-call | tf_op jit(solution)/shard_map/pallas_call | solution.py:200
  207.0 1.1 fusion.8
  208.2 2.0 copy.65.v_ref
  210.2 1.9 multiply_convert_fusion
  212.9 0.8 copy-done.2
  217.6 1.0 copy.63.q_ref
  219.0 1.0 copy.64.k_ref
  220.0 131.0 %shard_map.96 = (bf16[512,1024]{1,0:T(8,128)(2,1)}, f32[512,512]{1,0:T(8,128)}, f32[512,512]{1,0:T(8,128)}, f32[512,512]{1,0:T(8,128)}) custom-call(bf16[512,4096]{1,0:T(8,128)(2,1)} %tok_ref.3, bf16[512,512]{1,0:T(8,128)(2,1)} %copy.63.q_ref, bf16[512,512]{1,0:T(8,128)(2,1)} %copy.64.k_ref, bf16[512,512]{1,0:T(8,128)(2,1)} %copy.65.v_ref, ...), custom_call_target="tpu_custom_call" | custom-call | tf_op jit(solution)/shard_map/pallas_call | solution.py:350
  351.0 2.4 copy.112
  353.4 1.0 copy.113
  354.4 1.0 copy.114
  355.3 1.0 copy.115
  (77 shorter events, 9.3 us)
Async XLA Ops:
  0.6 1.4 copy-start.21
  1.9 139.1 %copy-start.8 = (bf16[4,128,256]{2,1,0:T(8,128)(2,1)}, bf16[4,128,256]{2,1,0:T(8,128)(2,1)S(1)}, u32[]{:S(2)}) copy-start(bf16[4,128,256]{2,1,0:T(8,128)(2,1)S(1)} %convert_element_type.96) | copy-start | bytes 786436
  135.4 3.6 %copy-start.11 = (bf16[512,512]{1,0:T(8,128)(2,1)S(1)}, bf16[512,512]{1,0:T(8,128)(2,1)}, u32[]{:S(2)}) copy-start(bf16[512,512]{1,0:T(8,128)(2,1)} %get-tuple-element.8) | copy-start | bytes 1572868
  136.8 0.8 copy-start.14
  138.8 2.2 copy-start.12
  139.0 2.0 copy-start.10
  172.0 5.2 %copy-start.16 = (bf16[1024,128]{1,0:T(8,128)(2,1)}, bf16[1024,128]{1,0:T(8,128)(2,1)S(1)}, u32[]{:S(2)}) copy-start(bf16[1024,128]{1,0:T(8,128)(2,1)S(1)} %slice.23) | copy-start | bytes 786436
  172.3 1.2 copy-start.6
  173.7 3.0 copy-start
  174.9 1.8 copy-start.4
  178.1 29.0 %copy-start.7 = (f32[4,512,128]{1,2,0:T(8,128)S(1)}, f32[4,512,128]{1,2,0:T(8,128)}, u32[]{:S(2)}) copy-start(f32[4,512,128]{1,2,0:T(8,128)} %fusion.27) | copy-start | bytes 3145732
  212.1 1.6 copy-start.2
  212.1 1.7 copy-start.5
  214.3 1.0 copy-start.1
  214.3 1.8 copy-start.3
  214.4 1.8 copy-start.17
  216.1 1.0 copy-start.9
  216.1 1.1 copy-start.15
  216.8 1.8 copy-start.13
  351.0 2.4 copy-start.20
  351.0 3.4 copy-start.19
  353.4 1.9 copy-start.18

commit v3 on v2

--- a/solution.py
+++ b/solution.py
@@ -159,44 +159,85 @@
     )(tokens, w_query, w_key, w_value)
 
 
-def scan_kernel(n, sign, x_ref, out_ref, total, send_buf, recv_buf, send_sem, recv_sem):
+PARTS = 4
+
+
+def scan_kernel(
+    n, sign, x_ref, out_ref, pair, pair_out, pair_in, chain_out, chain_in,
+    pair_send, pair_recv, chain_send, chain_recv,
+):
     me = lax.axis_index("seq")
-    steps = [1 << b for b in range((n - 1).bit_length())]
+    odd = lax.rem(me, 2)
+    partner = me + 1 - 2 * odd
+    half = lax.div(me, 2)
+    link = half if sign == 1 else n // 2 - 1 - half
+    has_before, has_after = link > 0, link < n // 2 - 1
+    before, after = lax.rem(me - 2 * sign + n, n), lax.rem(me + 2 * sign + n, n)
+    late = odd if sign == 1 else 1 - odd
     barrier = pltpu.get_barrier_semaphore()
-    for far in steps:
-        source = lax.rem(me - sign * far + n, n)
-        pl.semaphore_signal(barrier, inc=1, device_id={"seq": source}, device_id_type=MESH)
-    pl.semaphore_wait(barrier, len(steps))
-    total[...] = x_ref[...]
-    out_ref[...] = jnp.zeros_like(out_ref)
-    rank = me if sign == 1 else n - 1 - me
-    for place, far in enumerate(steps):
-        send_buf[place] = total[...].astype(jnp.bfloat16)
-        copy = pltpu.make_async_remote_copy(
-            src_ref=send_buf.at[place],
-            dst_ref=recv_buf.at[place],
-            send_sem=send_sem.at[place],
-            recv_sem=recv_sem.at[place],
-            device_id={"seq": lax.rem(me + sign * far + n, n)},
+    pl.semaphore_signal(barrier, inc=1, device_id={"seq": partner}, device_id_type=MESH)
+
+    @pl.when(has_before)
+    def _():
+        pl.semaphore_signal(barrier, inc=1, device_id={"seq": before}, device_id_type=MESH)
+
+    pl.semaphore_wait(barrier, 1 + lax.min(n // 2 - 1 - link, 1))
+
+    size = x_ref.shape[0] // PARTS
+    spans = tuple((part, slice(part * size, (part + 1) * size)) for part in range(PARTS))
+
+    def copy(kind, part):
+        source, target, send, recv, device = (
+            (pair_out, pair_in, pair_send, pair_recv, partner),
+            (chain_out, chain_in, chain_send, chain_recv, after),
+        )[kind]
+        return pltpu.make_async_remote_copy(
+            src_ref=source.at[part],
+            dst_ref=target.at[part],
+            send_sem=send.at[part],
+            recv_sem=recv.at[part],
+            device_id={"seq": device},
             device_id_type=MESH,
         )
-        copy.start()
-        copy.wait()
-        keep = jnp.broadcast_to(rank >= far, out_ref.shape)
-        got = jnp.where(keep, recv_buf[place].astype(jnp.float32), 0.0)
-        total[...] += got
-        out_ref[...] += got
+
+    for part, span in spans:
+        pair_out[part] = x_ref[span].astype(jnp.bfloat16)
+        copy(0, part).start()
+    keep = late.astype(jnp.float32)
+    for part, span in spans:
+        copy(0, part).wait()
+        got = pair_in[part].astype(jnp.float32)
+        pair[span] = x_ref[span] + got
+        out_ref[span] = got * keep
+
+        @pl.when(has_before)
+        def _():
+            copy(1, part).wait_recv()
+            chained = chain_in[part].astype(jnp.float32)
+            out_ref[span] += chained
+            pair[span] += chained
+
+        @pl.when(has_after)
+        def _():
+            chain_out[part] = pair[span].astype(jnp.bfloat16)
+            copy(1, part).start()
+
+    @pl.when(has_after)
+    def _():
+        for part, span in spans:
+            copy(1, part).wait_send()
 
 
 def carried(states, totals, n, sign):
     heads, features, size = states.shape
+    split = heads * features
     flat_totals = totals.reshape(-1, size)
     used = flat_totals.shape[0]
-    pad = (-(used)) % 16
+    pad = (-(split + used)) % (16 * PARTS)
     packed = jnp.concatenate(
         [states.reshape(-1, size), flat_totals, jnp.zeros((pad, size), jnp.float32)], 0
     )
-    steps = (n - 1).bit_length()
+    piece = (PARTS, packed.shape[0] // PARTS, size)
     out = pl.pallas_call(
         functools.partial(scan_kernel, n, sign),
         out_shape=jax.ShapeDtypeStruct(packed.shape, jnp.float32),
@@ -204,10 +245,8 @@
         out_specs=VMEM,
         scratch_shapes=[
             pltpu.VMEM(packed.shape, jnp.float32),
-            pltpu.VMEM((steps,) + packed.shape, jnp.bfloat16),
-            pltpu.VMEM((steps,) + packed.shape, jnp.bfloat16),
-            pltpu.SemaphoreType.DMA((steps,)),
-            pltpu.SemaphoreType.DMA((steps,)),
+            *[pltpu.VMEM(piece, jnp.bfloat16)] * 4,
+            *[pltpu.SemaphoreType.DMA((PARTS,))] * 4,
         ],
         compiler_params=pltpu.CompilerParams(
             collective_id=1 if sign == 1 else 2,
@@ -215,7 +254,6 @@
             vmem_limit_bytes=32 << 20,
         ),
     )(packed)
-    split = heads * features
     return out[:split].reshape(states.shape), out[split : split + used].reshape(totals.shape)
 
 

time: 357 us -> 338 us (0.947)
  Pallas kernels: 318 us -> 299 us
    pallas_call x2, Pallas kernels: 54.8 us -> 36 us  [carried(): pl.pallas_call(functools.partial(scan_kernel, n, sign), out_shape=jax.Sha...]
where the time goes in v3:
time: 338 us; the launch traced here: 337 us
  Pallas kernels  299 us (88%)
  matrix products  17.2 us (5%)
  local copies, waits for them, and re-layouts  16.8 us (5%)
    pallas_call x1, Pallas kernels, project(): pl.pallas_call(functools.partial(project_kernel, n), out_shape=(act, act,...  132 us
    pallas_call x1, Pallas kernels, gradients(): pl.pallas_call(functools.partial(grads_kernel, n, groups), out_shape=(jax...  131 us
    pallas_call x2, Pallas kernels, carried(): pl.pallas_call(functools.partial(scan_kernel, n, sign), out_shape=jax.Sha...  36 us
    dot_general x18, matrix products, ein(): jnp.einsum(spec, a.astype(jnp.bfloat16), b.astype(jnp.bfloat16), preferre...  17.2 us
    unnamed x48, local copies, waits for them, and re-layouts  8.81 us

profile of v3, /device:TPU:0, one launch (start us, length us, event | category | flops | bytes accessed | tf_op | source)
XLA Modules:
  0.0 337.4 jit_solution(9094241024225311761)
XLA Ops:
  0.7 1.1 convert_element_type.96
  2.0 1.2 copy.10
  3.2 132.3 %shard_map.93 = (bf16[512,512]{1,0:T(8,128)(2,1)}, bf16[512,512]{1,0:T(8,128)(2,1)}, bf16[512,512]{1,0:T(8,128)(2,1)}, bf16[2,8,512,768]{3,2,1,0:T(8,128)(2,1)}) custom-call(bf16[512,4096]{1,0:T(8,128)(2,1)} %tok_ref.3, bf16[512,512]{1,0:T(8,128)(2,1)} %wq_ref.1, bf16[512,512]{1,0:T(8,128)(2,1)} %wk_ref.1, bf16[512,512]{1,0:T(8,128)(2,1)} %wv_ref.1), custom_call_target="tpu_custom_call" | custom-call | flops 6442450944 | bytes 16777216 | tf_op jit(solution)/shard_map/pallas_call | solution.py:143
  135.4 1.3 copy.99
  137.6 1.3 copy.100
  139.0 2.0 fusion.33
  141.0 2.1 fusion.32
  143.1 1.5 fusion.21
  144.8 11.0 %shard_map.94 = f32[1088,128]{1,0:T(8,128)S(1)} custom-call(f32[1088,128]{1,0:T(8,128)S(1)} %maximum_maximum_fusion.x_ref), custom_call_target="tpu_custom_call" | custom-call | tf_op jit(solution)/shard_map/pallas_call | solution.py:241
  157.5 1.2 fusion.37
  158.7 1.8 fusion.27
  161.9 1.3 maximum_maximum_fusion.1.x_ref
  163.2 25.0 %shard_map.95 = f32[1088,128]{1,0:T(8,128)S(1)} custom-call(f32[1088,128]{1,0:T(8,128)S(1)} %maximum_maximum_fusion.1.x_ref), custom_call_target="tpu_custom_call" | custom-call | tf_op jit(solution)/shard_map/pallas_call | solution.py:241
  188.3 1.1 fusion.8
  189.5 2.0 copy.65.v_ref
  191.5 1.9 multiply_convert_fusion
  194.2 0.8 copy-done.2
  198.9 1.0 copy.63.q_ref
  200.3 1.0 copy.64.k_ref
  201.3 130.8 %shard_map.96 = (bf16[512,1024]{1,0:T(8,128)(2,1)}, f32[512,512]{1,0:T(8,128)}, f32[512,512]{1,0:T(8,128)}, f32[512,512]{1,0:T(8,128)}) custom-call(bf16[512,4096]{1,0:T(8,128)(2,1)} %tok_ref.3, bf16[512,512]{1,0:T(8,128)(2,1)} %copy.63.q_ref, bf16[512,512]{1,0:T(8,128)(2,1)} %copy.64.k_ref, bf16[512,512]{1,0:T(8,128)(2,1)} %copy.65.v_ref, ...), custom_call_target="tpu_custom_call" | custom-call | tf_op jit(solution)/shard_map/pallas_call | solution.py:388
  332.1 2.4 copy.112
  334.5 1.0 copy.113
  335.5 1.0 copy.114
  336.5 1.0 copy.115
  (77 shorter events, 9.3 us)
Async XLA Ops:
  0.6 1.4 copy-start.21
  1.9 139.1 %copy-start.8 = (bf16[4,128,256]{2,1,0:T(8,128)(2,1)}, bf16[4,128,256]{2,1,0:T(8,128)(2,1)S(1)}, u32[]{:S(2)}) copy-start(bf16[4,128,256]{2,1,0:T(8,128)(2,1)S(1)} %convert_element_type.96) | copy-start | bytes 786436
  135.4 3.6 %copy-start.11 = (bf16[512,512]{1,0:T(8,128)(2,1)S(1)}, bf16[512,512]{1,0:T(8,128)(2,1)}, u32[]{:S(2)}) copy-start(bf16[512,512]{1,0:T(8,128)(2,1)} %get-tuple-element.8) | copy-start | bytes 1572868
  136.8 0.8 copy-start.14
  138.8 2.2 copy-start.12
  139.0 2.0 copy-start.10
  155.8 5.3 %copy-start.16 = (bf16[1024,128]{1,0:T(8,128)(2,1)}, bf16[1024,128]{1,0:T(8,128)(2,1)S(1)}, u32[]{:S(2)}) copy-start(bf16[1024,128]{1,0:T(8,128)(2,1)S(1)} %slice.23) | copy-start | bytes 786436
  156.1 1.2 copy-start.6
  157.5 3.0 copy-start
  158.7 1.8 copy-start.4
  161.9 26.5 %copy-start.7 = (f32[4,512,128]{1,2,0:T(8,128)S(1)}, f32[4,512,128]{1,2,0:T(8,128)}, u32[]{:S(2)}) copy-start(f32[4,512,128]{1,2,0:T(8,128)} %fusion.27) | copy-start | bytes 3145732
  193.4 1.6 copy-start.2
  193.4 1.7 copy-start.5
  195.6 1.0 copy-start.1
  195.6 1.8 copy-start.3
  195.7 1.8 copy-start.17
  197.4 1.0 copy-start.9
  197.4 1.1 copy-start.15
  198.1 1.8 copy-start.13
  332.1 2.4 copy-start.20
  332.1 3.4 %copy-start.19 = (f32[512,512]{1,0:T(8,128)S(1)}, f32[512,512]{1,0:T(8,128)}, u32[]{:S(2)}) copy-start(f32[512,512]{1,0:T(8,128)} %get-tuple-element.35) | copy-start | bytes 3145732
  334.5 1.9 copy-start.18

commit v4 on v3

--- a/solution.py
+++ b/solution.py
@@ -159,7 +159,7 @@
     )(tokens, w_query, w_key, w_value)
 
 
-PARTS = 4
+PARTS = 8
 
 
 def scan_kernel(

time: 338 us -> 336 us (level)
  no operation moved by 1% of the time
where the time goes in v4:
time: 336 us
  Pallas kernels  298 us (89%)
  matrix products  17.2 us (5%)
  local copies, waits for them, and re-layouts  16.8 us (5%)
    pallas_call x1, Pallas kernels, project(): pl.pallas_call(functools.partial(project_kernel, n), out_shape=(act, act,...  132 us
    pallas_call x1, Pallas kernels, gradients(): pl.pallas_call(functools.partial(grads_kernel, n, groups), out_shape=(jax...  131 us
    pallas_call x2, Pallas kernels, carried(): pl.pallas_call(functools.partial(scan_kernel, n, sign), out_shape=jax.Sha...  34.4 us
    dot_general x18, matrix products, ein(): jnp.einsum(spec, a.astype(jnp.bfloat16), b.astype(jnp.bfloat16), preferre...  17.2 us
    unnamed x48, local copies, waits for them, and re-layouts  8.81 us

profile of v4, /device:TPU:0, one launch (start us, length us, event | category | flops | bytes accessed | tf_op | source)
XLA Modules:
  0.0 335.9 jit_solution(18312543095841185374)
XLA Ops:
  0.7 1.1 convert_element_type.96
  2.0 1.2 copy.10
  3.2 132.3 %shard_map.93 = (bf16[512,512]{1,0:T(8,128)(2,1)}, bf16[512,512]{1,0:T(8,128)(2,1)}, bf16[512,512]{1,0:T(8,128)(2,1)}, bf16[2,8,512,768]{3,2,1,0:T(8,128)(2,1)}) custom-call(bf16[512,4096]{1,0:T(8,128)(2,1)} %tok_ref.3, bf16[512,512]{1,0:T(8,128)(2,1)} %wq_ref.1, bf16[512,512]{1,0:T(8,128)(2,1)} %wk_ref.1, bf16[512,512]{1,0:T(8,128)(2,1)} %wv_ref.1), custom_call_target="tpu_custom_call" | custom-call | flops 6442450944 | bytes 16777216 | tf_op jit(solution)/shard_map/pallas_call | solution.py:143
  135.4 1.3 copy.99
  137.6 1.3 copy.100
  139.0 2.0 fusion.33
  141.0 2.1 fusion.32
  143.1 1.5 fusion.21
  144.8 10.9 %shard_map.94 = f32[1152,128]{1,0:T(8,128)S(1)} custom-call(f32[1152,128]{1,0:T(8,128)S(1)} %maximum_maximum_fusion.x_ref), custom_call_target="tpu_custom_call" | custom-call | tf_op jit(solution)/shard_map/pallas_call | solution.py:241
  157.4 1.2 fusion.37
  158.6 1.8 fusion.27
  161.8 1.4 maximum_maximum_fusion.1.x_ref
  163.2 23.4 %shard_map.95 = f32[1152,128]{1,0:T(8,128)S(1)} custom-call(f32[1152,128]{1,0:T(8,128)S(1)} %maximum_maximum_fusion.1.x_ref), custom_call_target="tpu_custom_call" | custom-call | tf_op jit(solution)/shard_map/pallas_call | solution.py:241
  186.7 1.1 fusion.8
  187.8 2.0 copy.65.v_ref
  189.9 1.9 multiply_convert_fusion
  192.5 0.8 copy-done.2
  197.3 1.0 copy.63.q_ref
  198.6 1.0 copy.64.k_ref
  199.6 130.9 %shard_map.96 = (bf16[512,1024]{1,0:T(8,128)(2,1)}, f32[512,512]{1,0:T(8,128)}, f32[512,512]{1,0:T(8,128)}, f32[512,512]{1,0:T(8,128)}) custom-call(bf16[512,4096]{1,0:T(8,128)(2,1)} %tok_ref.3, bf16[512,512]{1,0:T(8,128)(2,1)} %copy.63.q_ref, bf16[512,512]{1,0:T(8,128)(2,1)} %copy.64.k_ref, bf16[512,512]{1,0:T(8,128)(2,1)} %copy.65.v_ref, ...), custom_call_target="tpu_custom_call" | custom-call | tf_op jit(solution)/shard_map/pallas_call | solution.py:388
  330.5 2.4 copy.112
  332.9 1.0 copy.113
  333.9 1.0 copy.114
  334.9 1.0 copy.115
  (77 shorter events, 9.3 us)
Async XLA Ops:
  0.6 1.4 copy-start.21
  1.9 139.1 %copy-start.8 = (bf16[4,128,256]{2,1,0:T(8,128)(2,1)}, bf16[4,128,256]{2,1,0:T(8,128)(2,1)S(1)}, u32[]{:S(2)}) copy-start(bf16[4,128,256]{2,1,0:T(8,128)(2,1)S(1)} %convert_element_type.96) | copy-start | bytes 786436
  135.4 3.6 %copy-start.11 = (bf16[512,512]{1,0:T(8,128)(2,1)S(1)}, bf16[512,512]{1,0:T(8,128)(2,1)}, u32[]{:S(2)}) copy-start(bf16[512,512]{1,0:T(8,128)(2,1)} %get-tuple-element.8) | copy-start | bytes 1572868
  136.8 0.8 copy-start.14
  138.8 2.2 copy-start.12
  139.0 2.0 copy-start.10
  155.8 5.3 %copy-start.16 = (bf16[1024,128]{1,0:T(8,128)(2,1)}, bf16[1024,128]{1,0:T(8,128)(2,1)S(1)}, u32[]{:S(2)}) copy-start(bf16[1024,128]{1,0:T(8,128)(2,1)S(1)} %slice.23) | copy-start | bytes 786436
  156.0 1.2 copy-start.6
  157.4 3.0 copy-start
  158.6 1.8 copy-start.4
  161.8 24.9 %copy-start.7 = (f32[4,512,128]{1,2,0:T(8,128)S(1)}, f32[4,512,128]{1,2,0:T(8,128)}, u32[]{:S(2)}) copy-start(f32[4,512,128]{1,2,0:T(8,128)} %fusion.27) | copy-start | bytes 3145732
  191.8 1.6 copy-start.2
  191.8 1.7 copy-start.5
  194.0 1.0 copy-start.1
  194.0 1.8 copy-start.3
  194.0 1.8 copy-start.17
  195.8 1.0 copy-start.9
  195.8 1.1 copy-start.15
  196.4 1.8 copy-start.13
  330.5 2.4 copy-start.20
  330.5 3.4 %copy-start.19 = (f32[512,512]{1,0:T(8,128)S(1)}, f32[512,512]{1,0:T(8,128)}, u32[]{:S(2)}) copy-start(f32[512,512]{1,0:T(8,128)} %get-tuple-element.35) | copy-start | bytes 3145732
  332.9 1.9 copy-start.18
